TPU v7x, 32 devices: a whole 2x2x4 slice. The times are simulated.
32 devices in a mesh: section: 4 (over y, x), seq: 4 (over z), dp: 2 (over core).
Axes of the slice: x: 2, y: 2, z: 4, core: 2. Of those that a mesh axis runs over, the one named last changes fastest.
Arguments:
- queries: bfloat16 [8, 512, 1280], P(('section', 'dp'), 'seq'), may hold values from -5 to 5, as said below
- key_input: bfloat16 [8, 512, 1280], P(('section', 'dp'), 'seq'), may hold values from -5 to 5
- value_input: bfloat16 [8, 512, 1280], P(('section', 'dp'), 'seq'), may hold values from -6 to 6
- residual: bfloat16 [8, 512, 1280], P(('section', 'dp'), 'seq'), may hold values from -4 to 4
- segments: int32 [8, 512], P(('section', 'dp')), may hold values from 0 to 5, never falling along the last dimension, each value on 1 to 256 neighbouring positions
- out_weight: bfloat16 [1280, 1280], replicated, may hold values from -0.15625 to 0.15625
- cotangent: bfloat16 [8, 512, 1280], P(('section', 'dp'), 'seq'), may hold values from -6 to 6
Outputs:
- mixed_out: bfloat16 [8, 512, 1280], P(('section', 'dp'), 'seq')
- weight_grad: float32 [1280, 1280], P(('section', 'dp'))
Inputs may be any that keep to these rules, and one draw needn't show every extreme that they name: queries and key_input lie within -5 to 5.
All inputs are finite; a program needn't handle non-finite values.
Results may differ from a plain program's by a relative error of at most 0.015.
Values may be sent and summed in bfloat16 or wider, within the bound.
A program may use at most 64 MiB of HBM per device.

v0:
```python
import jax
import jax.numpy as jnp
from jax import lax
from jax.sharding import PartitionSpec as P

HEADS = 16


def passed_along(value, axis, steps):
    count = lax.axis_size(axis)
    leading, last = (max(0, -steps), min(count, count - steps))
    return lax.ppermute(value, axis, [(source, source + steps) for source in range(leading, last)])


def per_device(queries, key_input, value_input, residual, segments, out_weight, cotangent):
    row_count = queries.shape[1]
    feature_width = queries.shape[2]
    head_dim = feature_width // HEADS
    my_index = lax.axis_index("seq")
    total_len = segments.shape[1]
    stacked = jnp.stack([key_input[0], value_input[0]])
    pieces = []
    offsets = []
    pieces.append(stacked)
    offsets.append(my_index * row_count)
    for distance in (1, 2, -1, -2):
        pieces.append(passed_along(stacked, "seq", distance))
        offsets.append((my_index - distance) * row_count)
    gathered = jnp.concatenate(pieces, axis=1)
    key_pos = jnp.concatenate(
        [
            offset + jnp.arange(piece.shape[1], dtype=jnp.int32)
            for offset, piece in zip(offsets, pieces)
        ]
    )
    inside = (key_pos >= 0) & (key_pos < total_len)
    key_ids = jnp.take(segments[0], jnp.clip(key_pos, 0, total_len - 1))
    query_ids = lax.dynamic_slice_in_dim(segments[0], my_index * row_count, row_count, 0)
    usable = inside[None, :] & (key_ids[None, :] == query_ids[:, None])
    key_total = gathered.shape[1]
    query_heads = queries[0].reshape(row_count, HEADS, head_dim)
    key_heads = gathered[0].reshape(key_total, HEADS, head_dim)
    value_heads = gathered[1].reshape(key_total, HEADS, head_dim)
    scores = jnp.einsum(
        "qhd,khd->hqk", query_heads, key_heads, preferred_element_type=jnp.float32
    ) * head_dim ** (-0.5)
    scores = jnp.where(usable[None], scores, jnp.float32(-1e30))
    highest = jnp.max(scores, axis=-1, keepdims=True)
    expo = jnp.where(usable[None], jnp.exp(scores - highest), jnp.float32(0.0))
    probs = (expo / jnp.sum(expo, axis=-1, keepdims=True)).astype(jnp.bfloat16)
    attended = jnp.einsum("hqk,khd->qhd", probs, value_heads, preferred_element_type=jnp.float32)
    attended = attended.reshape(row_count, feature_width).astype(jnp.bfloat16)
    projected = lax.dot_general(
        attended, out_weight, (((1,), (1,)), ((), ())), preferred_element_type=jnp.float32
    )
    mixed_out = (residual[0].astype(jnp.float32) + projected).astype(jnp.bfloat16)[None]
    groups = lax.axis_size("section") * lax.axis_size("dp")
    grad_scale = 1.0 / float(groups * total_len) ** 0.5
    grad_input = cotangent[0]
    partial_value = (
        lax.dot_general(
            grad_input, attended, (((0,), (0,)), ((), ())), preferred_element_type=jnp.float32
        )
        * grad_scale
    )
    reduced = lax.psum_scatter(
        partial_value.astype(jnp.bfloat16), ("section", "dp"), scatter_dimension=0, tiled=True
    ).astype(jnp.float32)
    weight_grad = lax.psum(reduced, "seq")
    return (mixed_out, weight_grad)


def solution(mesh):
    in_specs = (
        P(("section", "dp"), "seq", None),
        P(("section", "dp"), "seq", None),
        P(("section", "dp"), "seq", None),
        P(("section", "dp"), "seq", None),
        P(("section", "dp"), None),
        P(),
        P(("section", "dp"), "seq", None),
    )
    out_specs = (P(("section", "dp"), "seq", None), P(("section", "dp"), None))
    return jax.shard_map(
        per_device, mesh=mesh, in_specs=in_specs, out_specs=out_specs, check_vma=False
    )
```

profile of v0, /device:TPU:0, one launch (start us, length us, event | category | flops | bytes accessed | tf_op | source)
XLA Modules:
  0.0 207.8 jit_solution(2780294254301819516)
XLA Ops:
  7.2 2.0 constant_dynamic-update-slice_fusion.1
  9.2 1.8 constant_dynamic-update-slice_fusion
  11.1 5.8 %collective-permute-start = (bf16[2,128,1280]{2,1,0:T(8,128)(2,1)}, bf16[2,128,1280]{2,1,0:T(8,128)(2,1)}, u32[]{:S(2)}, u32[]{:S(2)}) collective-permute-start(bf16[2,128,1280]{2,1,0:T(8,128)(2,1)} %get-tuple-element.10), channel_id=1, source_target_pairs={{0,2},{2,4},{4,6},{1,3},{3,5},{5,7},{8,10},{10,12},{12,14},{9,11},... | collective-permute-start | bytes 1966088 | tf_op jit(solution)/shard_map/ppermute | solution.py:12
  16.8 4.5 %collective-permute-start.1 = (bf16[2,128,1280]{2,1,0:T(8,128)(2,1)}, bf16[2,128,1280]{2,1,0:T(8,128)(2,1)}, u32[]{:S(2)}, u32[]{:S(2)}) collective-permute-start(bf16[2,128,1280]{2,1,0:T(8,128)(2,1)} %get-tuple-element.10), channel_id=1, source_target_pairs={{0,4},{2,6},{1,5},{3,7},{8,12},{10,14},{9,13},{11,15},{16,20},{18,... | collective-permute-start | bytes 1966088 | tf_op jit(solution)/shard_map/ppermute | solution.py:12
  24.1 1.9 copy.21
  26.7 4.3 %gather_fusion = s32[640]{0:T(1024)S(1)} fusion(s32[512]{0:T(512)S(1)} %bitcast.49, s32[1024]{0:T(1024)S(1)} %pad_clamp_fusion), kind=kCustom, calls=%fused_computation | custom fusion | bytes 7680 | tf_op jit(solution)/shard_map/jit(_take)/gather | solution.py:37
  31.4 2.0 constant_dynamic-update-slice_fusion.5
  33.4 11.0 %collective-permute-done.1 = bf16[2,128,1280]{2,1,0:T(8,128)(2,1)} collective-permute-done((bf16[2,128,1280]{2,1,0:T(8,128)(2,1)}, bf16[2,128,1280]{2,1,0:T(8,128)(2,1)}, u32[]{:S(2)}, u32[]{:S(2)}) %collective-permute-start.1) | collective-permute-done | bytes 655392 | tf_op jit(solution)/shard_map/ppermute | solution.py:12
  44.4 2.0 constant_dynamic-update-slice_fusion.4
  46.3 2.0 constant_dynamic-update-slice_fusion.3
  48.3 18.3 %collective-permute-done.3 = bf16[2,128,1280]{2,1,0:T(8,128)(2,1)} collective-permute-done((bf16[2,128,1280]{2,1,0:T(8,128)(2,1)}, bf16[2,128,1280]{2,1,0:T(8,128)(2,1)}, u32[]{:S(2)}, u32[]{:S(2)}) %collective-permute-start.3) | collective-permute-done | bytes 655392 | tf_op jit(solution)/shard_map/ppermute | solution.py:12
  66.6 2.0 constant_dynamic-update-slice_fusion.2
  68.6 3.8 %fusion.17 = (bf16[1,640,1280]{2,1,0:T(8,128)(2,1)}, bf16[1,640,1280]{2,1,0:T(8,128)(2,1)}) fusion(bf16[2,640,1280]{2,1,0:T(8,128)(2,1)} %constant_dynamic-update-slice_fusion.2), kind=kLoop, calls=%fused_computation.52 | loop fusion | bytes 6553600 | tf_op jit(solution)/shard_map/slice | solution.py:42
  72.4 3.5 %copy.19 = bf16[1,640,1280]{1,2,0:T(8,128)(2,1)} copy(bf16[1,640,1280]{2,1,0:T(8,128)(2,1)} %get-tuple-element.9) | data formatting | bytes 3276800 | tf_op jit(solution)/shard_map/slice | solution.py:43
  76.0 3.6 %copy.20 = bf16[1,640,1280]{1,2,0:T(8,128)(2,1)} copy(bf16[1,640,1280]{2,1,0:T(8,128)(2,1)} %get-tuple-element.8) | data formatting | bytes 3276800 | tf_op jit(solution)/shard_map/slice | solution.py:42
  79.5 6.1 %fusion.18 = (f32[16,128]{1,0:T(8,128)S(1)}, f32[16,128,640]{1,2,0:T(8,128)}) fusion(pred[128,640]{0,1:T(8,128)(4,1)S(1)} %compare_and_fusion, bf16[640,16,80]{0,2,1:T(8,128)(2,1)} %bitcast.51, bf16[128,16,80]{0,2,1:T(8,128)(2,1)} %bitcast.54), kind=kOutput, calls=%fused_computation.53 | convolution fusion | flops 216269440 | bytes 7299072 | tf_op jit(solution)/shard_map/sub | solution.py:49
  85.6 3.7 %fusion.10 = bf16[16,80,128]{2,1,0:T(8,128)(2,1)S(1)} fusion(bf16[640,16,80]{0,2,1:T(8,128)(2,1)} %bitcast.50, f32[16,128,640]{1,2,0:T(8,128)} %get-tuple-element.15, f32[16,128]{1,0:T(8,128)S(1)} %get-tuple-element.14), kind=kOutput, calls=%fused_computation.16 | convolution fusion | flops 212500480 | bytes 7217152 | tf_op jit(solution)/shard_map/hqk,khd->qhd/dot_general | solution.py:51
  90.0 2.7 %fusion.2 = bf16[1280,1280]{0,1:T(8,128)(2,1)} fusion(bf16[128,1280]{0,1:T(8,128)(2,1)S(1)} %bitcast.52, bf16[1,128,1280]{2,1,0:T(8,128)(2,1)S(1)} %copy-done.3), kind=kOutput, calls=%fused_computation.4 | convolution fusion | flops 422707200 | bytes 3932160 | tf_op jit(solution)/shard_map/dot_general | solution.py:61
  92.8 5.6 %copy.25 = bf16[1280,1280]{1,0:T(8,128)(2,1)} copy(bf16[1280,1280]{0,1:T(8,128)(2,1)} %fusion.2) | data formatting | bytes 6553600
  98.4 3.0 %fusion.9 = bf16[1,128,1280]{2,1,0:T(8,128)(2,1)} fusion(bf16[128,1280]{0,1:T(8,128)(2,1)} %bitcast.53, bf16[1280,1280]{1,0:T(8,128)(2,1)S(1)} %copy-done, bf16[1,128,1280]{2,1,0:T(8,128)(2,1)} %param.10), kind=kOutput, calls=%fused_computation.15 | convolution fusion | flops 419921920 | bytes 4259840 | tf_op jit(solution)/shard_map/dot_general | solution.py:53
  101.4 42.2 %reduce-scatter.4.cloned.1.call-done = bf16[160,1280]{1,0:T(8,128)(2,1)} async-done(((bf16[1280,1280]{1,0:T(8,128)(2,1)}), bf16[160,1280]{1,0:T(8,128)(2,1)}) %reduce-scatter.4.cloned.1.call-update) | async-done | bytes 409616
  143.7 2.1 copy.26
  145.7 52.7 %all-reduce.1 = f32[160,1280]{0,1:T(8,128)} all-reduce(bf16[160,1280]{0,1:T(8,128)(2,1)} %copy.26), channel_id=1, replica_groups=mesh['section'=4,'seq'=4,'dp'=2] {'seq'}, use_global_device_ids=true, to_apply=%region_3.4 | all-reduce | flops 204800 | bytes 1228800 | tf_op jit(solution)/shard_map/psum | solution.py:69
  198.4 2.6 %copy.23 = f32[160,1280]{1,0:T(8,128)} copy(f32[160,1280]{0,1:T(8,128)} %all-reduce.1) | data formatting | bytes 1638400
  (31 shorter events, 4.6 us)
Async XLA Ops:
  7.2 91.3 %copy-start = (bf16[1280,1280]{1,0:T(8,128)(2,1)S(1)}, bf16[1280,1280]{1,0:T(8,128)(2,1)}, u32[]{:S(2)}) copy-start(bf16[1280,1280]{1,0:T(8,128)(2,1)} %param.12) | copy-start | bytes 9830404
  7.2 19.5 %copy-start.1 = (s32[1,512]{1,0:T(1,128)S(1)}, s32[1,512]{1,0:T(1,128)}, u32[]{:S(2)}) copy-start(s32[1,512]{1,0:T(1,128)} %param.11) | copy-start | bytes 6148
  7.2 136.5 %reduce-scatter.4.cloned.1.call-start = ((), (), s32[]{:S(2)}) async-start(), calls=%async_computation.1 | async-start | bytes 3686400
  11.1 20.4 %collective-permute-start = (bf16[2,128,1280]{2,1,0:T(8,128)(2,1)}, bf16[2,128,1280]{2,1,0:T(8,128)(2,1)}, u32[]{:S(2)}, u32[]{:S(2)}) collective-permute-start(bf16[2,128,1280]{2,1,0:T(8,128)(2,1)} %get-tuple-element.10), channel_id=1, source_target_pairs={{0,2},{2,4},{4,6},{1,3},{3,5},{5,7},{8,10},{10,12},{12,14},{9,11},... | collective-permute-start | bytes 1966088 | tf_op jit(solution)/shard_map/ppermute | solution.py:12
  16.8 27.5 %collective-permute-start.1 = (bf16[2,128,1280]{2,1,0:T(8,128)(2,1)}, bf16[2,128,1280]{2,1,0:T(8,128)(2,1)}, u32[]{:S(2)}, u32[]{:S(2)}) collective-permute-start(bf16[2,128,1280]{2,1,0:T(8,128)(2,1)} %get-tuple-element.10), channel_id=1, source_target_pairs={{0,4},{2,6},{1,5},{3,7},{8,12},{10,14},{9,13},{11,15},{16,20},{18,... | collective-permute-start | bytes 1966088 | tf_op jit(solution)/shard_map/ppermute | solution.py:12
  21.3 25.0 %collective-permute-start.2 = (bf16[2,128,1280]{2,1,0:T(8,128)(2,1)}, bf16[2,128,1280]{2,1,0:T(8,128)(2,1)}, u32[]{:S(2)}, u32[]{:S(2)}) collective-permute-start(bf16[2,128,1280]{2,1,0:T(8,128)(2,1)} %get-tuple-element.10), channel_id=1, source_target_pairs={{2,0},{4,2},{6,4},{3,1},{5,3},{7,5},{10,8},{12,10},{14,12},{11,9},... | collective-permute-start | bytes 1966088 | tf_op jit(solution)/shard_map/ppermute | solution.py:12
  22.6 44.0 %collective-permute-start.3 = (bf16[2,128,1280]{2,1,0:T(8,128)(2,1)}, bf16[2,128,1280]{2,1,0:T(8,128)(2,1)}, u32[]{:S(2)}, u32[]{:S(2)}) collective-permute-start(bf16[2,128,1280]{2,1,0:T(8,128)(2,1)} %get-tuple-element.10), channel_id=1, source_target_pairs={{4,0},{6,2},{5,1},{7,3},{12,8},{14,10},{13,9},{15,11},{20,16},{22,... | collective-permute-start | bytes 1966088 | tf_op jit(solution)/shard_map/ppermute | solution.py:12
  85.6 4.4 %copy-start.3 = (bf16[1,128,1280]{2,1,0:T(8,128)(2,1)S(1)}, bf16[1,128,1280]{2,1,0:T(8,128)(2,1)}, u32[]{:S(2)}) copy-start(bf16[1,128,1280]{2,1,0:T(8,128)(2,1)} %param.13) | copy-start | bytes 983044
  89.3 0.7 copy-start.2
Sparse Core Ops, SparseCore 0:
  98.6 45.0 reduce-scatter.3
where the time goes:
time: 209 us; the launch traced here: 208 us
  waiting for transfers between devices  71.7 us (34%)
  blocking collectives  52.7 us (25%)
  local copies, waits for them, and re-layouts  40.5 us (19%)
  matrix products  15.5 us (7%)
  between operations  14.2 us (7%)
  starting transfers between devices  12.9 us (6%)
    psum x1, blocking collectives, per_device(): weight_grad = lax.psum(reduced, 'seq')  52.7 us
    unnamed x2, waiting for transfers between devices  42.2 us
    ppermute x4, waiting for transfers between devices, passed_along(): lax.ppermute(value, axis, [(source, source + steps) for source in range(l...  29.5 us
    unnamed x16, local copies, waits for them, and re-layouts  20.8 us
    ppermute x4, starting transfers between devices, passed_along(): lax.ppermute(value, axis, [(source, source + steps) for source in range(l...  12.9 us
    slice x2, local copies, waits for them, and re-layouts, per_device(): key_heads = gathered[0].reshape(key_total, HEADS, head_dim)  7.38 us
    sub x1, matrix products, per_device(): expo = jnp.where(usable[None], jnp.exp(scores - highest), jnp.float32(0.0))  6.07 us
    gather x1, local copies, waits for them, and re-layouts, per_device(): key_ids = jnp.take(segments[0], jnp.clip(key_pos, 0, total_len - 1))  4.3 us
  transfers between devices with their start and end apart: 5, of which 4 were waited for; matrix products, arithmetic and copies ran while one was open for 8% of the time, Pallas kernels for 0%

commit v1 on v0

v1 whole, which is shorter than its diff:
```python
import functools
import math

import jax
import jax.numpy as jnp
from jax import lax
from jax.experimental import pallas as pl
from jax.experimental.pallas import tpu as pltpu
from jax.sharding import PartitionSpec as P

HEADS = 16
MOST = 256
LANES = 128
MESH = pl.DeviceIdType.MESH


def body(dims, q_hbm, k_hbm, v_hbm, res_hbm, seg_ref, w_hbm, cot_hbm, mix_ref, wg_ref,
         q, res, cot, w, kbuf, vbuf, cot_t, bias, att, mix, part, dp_in, pair, sec_in, acc,
         chain_out, chain_in,
         local_sem, kv_send, kv_recv, dp_send, dp_recv, sec_send, sec_recv, ch_send, ch_recv):
    N, S, D, rows, width, C, reach, R, subs = dims
    halves = width // C
    head_dim = width // HEADS
    half_heads = C // head_dim
    slots = 2 * reach + 1
    me, sec, core = lax.axis_index("seq"), lax.axis_index("section"), lax.axis_index("dp")
    towards = (1, -1)

    def can_send(direction):
        return (me < N - 1) if direction > 0 else (me > 0)

    def can_take(direction, hops):
        return (me >= hops) if direction > 0 else (me < N - hops)

    barrier = pltpu.get_barrier_semaphore()
    for direction in towards:
        @pl.when(can_send(direction))
        def _():
            pl.semaphore_signal(barrier, inc=1, device_id={"seq": me + direction}, device_id_type=MESH)
    for o in range(1, S):
        pl.semaphore_signal(barrier, inc=1, device_id={"section": lax.rem(sec + o, S)}, device_id_type=MESH)
    for o in range(1, D):
        pl.semaphore_signal(barrier, inc=1, device_id={"dp": lax.rem(core + o, D)}, device_id_type=MESH)

    own_rows = pl.ds(reach * rows, rows)
    locals_ = [
        pltpu.make_async_copy(src, dst, local_sem.at[i])
        for i, (src, dst) in enumerate((
            (cot_hbm.at[0], cot), (q_hbm.at[0], q),
            (k_hbm.at[0], kbuf.at[own_rows]), (v_hbm.at[0], vbuf.at[own_rows]),
            (res_hbm.at[0], res), (w_hbm, w)))
    ]
    for copy in locals_:
        copy.start()

    beside = (me < N - 1).astype(jnp.int32) + (me > 0).astype(jnp.int32)
    pl.semaphore_wait(barrier, beside + (S - 1) + (D - 1))

    def kv_copy(side, hop, c, kind):
        direction = towards[side]
        cols = pl.ds(c * C, C)
        buf = (kbuf, vbuf)[kind]
        if hop == 1:
            src = (k_hbm, v_hbm)[kind].at[0, :, cols]
        else:
            src = buf.at[pl.ds((reach - direction * (hop - 1)) * rows, rows), cols]
        return pltpu.make_async_remote_copy(
            src_ref=src, dst_ref=buf.at[pl.ds((reach - direction * hop) * rows, rows), cols],
            send_sem=kv_send.at[side, hop - 1, c, kind], recv_sem=kv_recv.at[side, hop - 1, c, kind],
            device_id={"seq": me + direction}, device_id_type=MESH)

    def kv_sends(side, hop):
        return can_send(towards[side]) & can_take(towards[side], hop - 1)

    for c in range(halves):
        for side in range(2):
            @pl.when(kv_sends(side, 1))
            def _():
                for kind in range(2):
                    kv_copy(side, 1, c, kind).start()

    for side in range(2):
        for hop in range(1, reach + 1):
            @pl.when(jnp.logical_not(can_take(towards[side], hop)))
            def _():
                at = pl.ds((reach - towards[side] * hop) * rows, rows)
                kbuf[at, :] = jnp.zeros((rows, width), kbuf.dtype)
                vbuf[at, :] = jnp.zeros((rows, width), vbuf.dtype)

    def ids_at(block):
        return seg_ref[:, pl.ds(pl.multiple_of(block * rows, rows), rows)].astype(jnp.float32)

    own_ids = jnp.transpose(jnp.broadcast_to(ids_at(me), (rows, rows)))
    for slot in range(slots):
        block = me + (slot - reach)
        inside = (block >= 0) & (block < N)
        ids = ids_at(jnp.clip(block, 0, N - 1))
        ids = jnp.where(inside, ids, jnp.float32(-1.0))
        bias[:, slot * rows:(slot + 1) * rows] = jnp.where(
            own_ids == jnp.broadcast_to(ids, (rows, rows)), jnp.float32(0.0), jnp.float32(-1e30))

    locals_[0].wait()
    cot_t[...] = jnp.transpose(cot[...].astype(jnp.float32)).astype(cot_t.dtype)
    att[...] = jnp.zeros_like(att)

    for hop in range(2, reach + 1):
        for c in range(halves):
            for side in range(2):
                @pl.when(can_take(towards[side], hop - 1))
                def _():
                    for kind in range(2):
                        kv_copy(side, hop - 1, c, kind).wait_recv()

                @pl.when(kv_sends(side, hop))
                def _():
                    for kind in range(2):
                        kv_copy(side, hop, c, kind).start()
    for copy in locals_[1:4]:
        copy.wait()

    fold = head_dim ** -0.5 * math.log2(math.e)

    def attention(c):
        for side in range(2):
            @pl.when(can_take(towards[side], reach))
            def _():
                for kind in range(2):
                    kv_copy(side, reach, c, kind).wait_recv()
        for head in range(c * half_heads, (c + 1) * half_heads):
            first, last = head * head_dim, (head + 1) * head_dim
            lo, hi = first // LANES * LANES, -(-last // LANES) * LANES
            lane = lax.broadcasted_iota(jnp.int32, (1, hi - lo), 1) + lo
            mine = jnp.where((lane >= first) & (lane < last), jnp.float32(1.0), jnp.float32(0.0))
            query = q[:, lo:hi] * mine.astype(jnp.bfloat16)
            scores = lax.dot_general(query, kbuf[:, lo:hi], (((1,), (1,)), ((), ())),
                                     preferred_element_type=jnp.float32)
            scores = scores * fold + bias[...]
            expo = jnp.exp2(scores - jnp.max(scores, axis=-1, keepdims=True))
            total = jnp.sum(expo, axis=-1, keepdims=True)
            out = jnp.dot(expo.astype(jnp.bfloat16), vbuf[:, lo:hi], preferred_element_type=jnp.float32)
            att[:, lo:hi] += out * (mine / total)

    def dp_copy(c, o):
        peer = lax.rem(core + o, D)
        return pltpu.make_async_remote_copy(
            src_ref=part.at[c, peer], dst_ref=dp_in.at[c, o - 1],
            send_sem=dp_send.at[c, o - 1], recv_sem=dp_recv.at[c, o - 1],
            device_id={"dp": peer}, device_id_type=MESH)

    def sec_copy(c, o):
        peer = lax.rem(sec + o, S)
        return pltpu.make_async_remote_copy(
            src_ref=pair.at[c, peer], dst_ref=sec_in.at[c, o - 1],
            send_sem=sec_send.at[c, o - 1], recv_sem=sec_recv.at[c, o - 1],
            device_id={"section": peer}, device_id_type=MESH)

    grad_scale = 1.0 / float(S * D * N * rows) ** 0.5
    tile = max(1, 640 // R)

    def partials(c):
        here = att[:, c * C:(c + 1) * C].astype(jnp.bfloat16)
        groups = S * D
        for at in range(0, groups, tile):
            count = min(tile, groups - at)
            value = jnp.dot(cot_t[at * R:(at + count) * R, :], here,
                            preferred_element_type=jnp.float32) * grad_scale
            for j in range(count):
                group = at + j
                part[c, group % D, group // D] = value[j * R:(j + 1) * R].astype(part.dtype)
        for o in range(1, D):
            dp_copy(c, o).start()

    def pair_up(c):
        for o in range(1, D):
            dp_copy(c, o).wait_recv()
        for o in [*range(1, S), 0]:
            peer = lax.rem(sec + o, S)
            value = part[c, core, peer].astype(jnp.float32)
            for p in range(1, D):
                value = value + dp_in[c, p - 1, peer].astype(jnp.float32)
            if o:
                pair[c, peer] = value.astype(pair.dtype)
                sec_copy(c, o).start()
            else:
                acc[c] = value

    edges = [(C // LANES * i // subs * LANES, C // LANES * (i + 1) // subs * LANES) for i in range(subs)]

    def chain_copy(side, c, s):
        cols = pl.ds(edges[s][0], edges[s][1] - edges[s][0])
        return pltpu.make_async_remote_copy(
            src_ref=chain_out.at[side, c, :, cols], dst_ref=chain_in.at[side, c, :, cols],
            send_sem=ch_send.at[side, c, s], recv_sem=ch_recv.at[side, c, s],
            device_id={"seq": me + towards[side]}, device_id_type=MESH)

    def chain_start(c):
        for o in range(1, S):
            sec_copy(c, o).wait_recv()
        for s, (lo, hi) in enumerate(edges):
            value = acc[c, :, lo:hi]
            for o in range(1, S):
                value = value + sec_in[c, o - 1, :, lo:hi].astype(jnp.float32)
            acc[c, :, lo:hi] = value
            for side in range(2):
                @pl.when(can_send(towards[side]) & jnp.logical_not(can_take(towards[side], 1)))
                def _():
                    chain_out[side, c, :, lo:hi] = acc[c, :, lo:hi].astype(chain_out.dtype)
                    chain_copy(side, c, s).start()
            wg_ref[:, c * C + lo:c * C + hi] = value

    def chain_rest(c):
        for s, (lo, hi) in enumerate(edges):
            for turn in range(2):
                for side in range(2):
                    near = (me * 2 < N) if side == 0 else (me * 2 >= N)
                    now = near if turn == 0 else jnp.logical_not(near)

                    @pl.when(now & can_take(towards[side], 1))
                    def _():
                        chain_copy(side, c, s).wait_recv()
                        came = chain_in[side, c, :, lo:hi].astype(jnp.float32)

                        @pl.when(can_send(towards[side]))
                        def _():
                            chain_out[side, c, :, lo:hi] = (acc[c, :, lo:hi] + came).astype(chain_out.dtype)
                            chain_copy(side, c, s).start()
                        wg_ref[:, c * C + lo:c * C + hi] += came

    def project(c):
        here = att[:, c * C:(c + 1) * C].astype(jnp.bfloat16)
        value = lax.dot_general(here, w[:, c * C:(c + 1) * C], (((1,), (1,)), ((), ())),
                                preferred_element_type=jnp.float32)
        if c == 0:
            mix[...] = res[...].astype(jnp.float32) + value
        elif c < halves - 1:
            mix[...] += value
        if c == halves - 1:
            mix_ref[0] = (mix[...] + (value if c else 0.0)).astype(mix_ref.dtype)

    for c in range(halves):
        attention(c)
        partials(c)
        if c == 0:
            for copy in locals_[4:]:
                copy.wait()
        if c < halves - 1:
            project(c)
        pair_up(c)
    project(halves - 1)
    for c in range(halves):
        chain_start(c)
        chain_rest(c)

    for c in range(halves):
        for side in range(2):
            for hop in range(1, reach + 1):
                @pl.when(kv_sends(side, hop))
                def _():
                    for kind in range(2):
                        kv_copy(side, hop, c, kind).wait_send()

            @pl.when(can_send(towards[side]))
            def _():
                for s in range(subs):
                    chain_copy(side, c, s).wait_send()
        for o in range(1, D):
            dp_copy(c, o).wait_send()
        for o in range(1, S):
            sec_copy(c, o).wait_send()


def solution(mesh):
    N, S, D = mesh.shape["seq"], mesh.shape["section"], mesh.shape["dp"]

    def per_device(queries, key_input, value_input, residual, segments, out_weight, cotangent):
        rows, width = queries.shape[1], queries.shape[2]
        head_dim = width // HEADS
        C = math.lcm(head_dim, LANES)
        halves = width // C
        reach = min(-(-(MOST - 1) // rows), N - 1)
        R = width // (S * D)
        subs = 2
        link = jnp.bfloat16 if N <= 8 else jnp.float32
        bf, f32 = jnp.bfloat16, jnp.float32
        span = (2 * reach + 1) * rows
        others, cores = max(1, S - 1), max(1, D - 1)
        dma = pltpu.SemaphoreType.DMA
        anywhere = pl.BlockSpec(memory_space=pl.ANY)
        vmem = pl.BlockSpec(memory_space=pltpu.VMEM)
        return pl.pallas_call(
            functools.partial(body, (N, S, D, rows, width, C, reach, R, subs)),
            out_shape=(jax.ShapeDtypeStruct((1, rows, width), bf), jax.ShapeDtypeStruct((R, width), f32)),
            in_specs=[anywhere] * 4 + [vmem] + [anywhere] * 2,
            out_specs=(vmem, vmem),
            scratch_shapes=[
                pltpu.VMEM((rows, width), bf), pltpu.VMEM((rows, width), bf), pltpu.VMEM((rows, width), bf),
                pltpu.VMEM((width, width), bf),
                pltpu.VMEM((span, width), bf), pltpu.VMEM((span, width), bf),
                pltpu.VMEM((width, rows), bf), pltpu.VMEM((rows, span), f32),
                pltpu.VMEM((rows, width), f32), pltpu.VMEM((rows, width), f32),
                pltpu.VMEM((halves, D, S, R, C), bf), pltpu.VMEM((halves, cores, S, R, C), bf),
                pltpu.VMEM((halves, S, R, C), bf), pltpu.VMEM((halves, others, R, C), bf),
                pltpu.VMEM((halves, R, C), f32),
                pltpu.VMEM((2, halves, R, C), link), pltpu.VMEM((2, halves, R, C), link),
                dma((6,)), dma((2, reach, halves, 2)), dma((2, reach, halves, 2)),
                dma((halves, cores)), dma((halves, cores)), dma((halves, others)), dma((halves, others)),
                dma((2, halves, subs)), dma((2, halves, subs)),
            ],
            compiler_params=pltpu.CompilerParams(
                collective_id=0, has_side_effects=True, vmem_limit_bytes=48 * 1024 * 1024),
        )(queries, key_input, value_input, residual, segments, out_weight, cotangent)

    rows_spec = P(("section", "dp"), "seq", None)
    in_specs = (rows_spec, rows_spec, rows_spec, rows_spec, P(("section", "dp"), None), P(), rows_spec)
    return jax.shard_map(per_device, mesh=mesh, in_specs=in_specs,
                         out_specs=(rows_spec, P(("section", "dp"), None)), check_vma=False)
```

time: 209 us -> 83.5 us (0.40)
  Pallas kernels: 0 us -> 73.4 us
  waiting for transfers between devices: 71.7 us -> 0 us
  blocking collectives: 52.7 us -> 0 us
  local copies, waits for them, and re-layouts: 40.5 us -> 9.08 us
  matrix products: 15.5 us -> 0 us
  between operations: 14.2 us -> 0.66 us
  starting transfers between devices: 12.9 us -> 0 us
    pallas_call x0 -> x1, Pallas kernels: none -> 73.4 us  [per_device(): pl.pallas_call(functools.partial(body, (N, S, D, rows, width, C, reach, R...]
    psum x1 -> x0, blocking collectives: 52.7 us -> none  [per_device(): weight_grad = lax.psum(reduced, 'seq')]
    unnamed x2 -> x0, waiting for transfers between devices: 42.2 us -> none
    ppermute x4 -> x0, waiting for transfers between devices: 29.5 us -> none  [passed_along(): lax.ppermute(value, axis, [(source, source + steps) for source in range(l...]
    ppermute x4 -> x0, starting transfers between devices: 12.9 us -> none  [passed_along(): lax.ppermute(value, axis, [(source, source + steps) for source in range(l...]
    unnamed x16, local copies, waits for them, and re-layouts: 20.8 us -> 9.08 us
    slice x3 -> x0, local copies, waits for them, and re-layouts: 10.9 us -> none  [the longest x2 7.38 us: per_device(): key_heads = gathered[0].reshape(key_total, HEADS, head_dim)]
    dot_general x3 -> x0, matrix products: 9.44 us -> none  [the longest x1 3.71 us: per_device(): jnp.einsum('hqk,khd->qhd', probs, value_heads, preferred_element_type=jnp...]
  transfers between devices with their start and end apart: 5 -> 0, of which waited for: 4 -> 0; matrix products, arithmetic and copies ran while one was open for 8% -> 0% of each run, Pallas kernels for 0% -> 0%
where the time goes in v1:
time: 83.5 us; the launch traced here: 83.1 us
  Pallas kernels  73.4 us (88%)
  local copies, waits for them, and re-layouts  9.08 us (11%)
    pallas_call x1, Pallas kernels, per_device(): pl.pallas_call(functools.partial(body, (N, S, D, rows, width, C, reach, R...  73.4 us
    unnamed x16, local copies, waits for them, and re-layouts  9.08 us

profile of v1, /device:TPU:0, one launch (start us, length us, event | category | flops | bytes accessed | tf_op | source)
XLA Modules:
  0.0 83.1 jit_solution(15707330272947489252)
XLA Ops:
  0.6 0.0 copy-start
  0.6 1.9 %copy-done = bf16[1280,1280]{1,0:T(8,128)(2,1)S(1)} copy-done((bf16[1280,1280]{1,0:T(8,128)(2,1)S(1)}, bf16[1280,1280]{1,0:T(8,128)(2,1)}, u32[]{:S(2)}) %copy-start) | copy-done | bytes 3276824
  2.6 0.0 copy-start.1
  2.6 1.0 %copy-done.1 = bf16[1,128,1280]{2,1,0:T(8,128)(2,1)S(1)} copy-done((bf16[1,128,1280]{2,1,0:T(8,128)(2,1)S(1)}, bf16[1,128,1280]{2,1,0:T(8,128)(2,1)}, u32[]{:S(2)}) %copy-start.1) | copy-done | bytes 327704
  3.5 0.0 copy-start.2
  3.5 1.0 %copy-done.2 = bf16[1,128,1280]{2,1,0:T(8,128)(2,1)S(1)} copy-done((bf16[1,128,1280]{2,1,0:T(8,128)(2,1)S(1)}, bf16[1,128,1280]{2,1,0:T(8,128)(2,1)}, u32[]{:S(2)}) %copy-start.2) | copy-done | bytes 327704
  4.5 0.0 copy-start.3
  4.5 1.0 %copy-done.3 = bf16[1,128,1280]{2,1,0:T(8,128)(2,1)S(1)} copy-done((bf16[1,128,1280]{2,1,0:T(8,128)(2,1)S(1)}, bf16[1,128,1280]{2,1,0:T(8,128)(2,1)}, u32[]{:S(2)}) %copy-start.3) | copy-done | bytes 327704
  5.5 0.0 copy-start.4
  5.5 1.0 %copy-done.4 = bf16[1,128,1280]{2,1,0:T(8,128)(2,1)S(1)} copy-done((bf16[1,128,1280]{2,1,0:T(8,128)(2,1)S(1)}, bf16[1,128,1280]{2,1,0:T(8,128)(2,1)}, u32[]{:S(2)}) %copy-start.4) | copy-done | bytes 327704
  6.5 0.0 copy-start.5
  6.5 1.0 %copy-done.5 = bf16[1,128,1280]{2,1,0:T(8,128)(2,1)S(1)} copy-done((bf16[1,128,1280]{2,1,0:T(8,128)(2,1)S(1)}, bf16[1,128,1280]{2,1,0:T(8,128)(2,1)}, u32[]{:S(2)}) %copy-start.5) | copy-done | bytes 327704
  7.4 0.0 copy-start.6
  7.4 0.7 copy-done.6
  8.1 73.4 %shard_map.86 = (bf16[1,128,1280]{2,1,0:T(8,128)(2,1)S(1)}, f32[160,1280]{1,0:T(8,128)S(1)}) custom-call(bf16[1,128,1280]{2,1,0:T(8,128)(2,1)S(1)} %copy-done.1, bf16[1,128,1280]{2,1,0:T(8,128)(2,1)S(1)} %copy-done.2, bf16[1,128,1280]{2,1,0:T(8,128)(2,1)S(1)} %copy-done.3, bf16[1,128,1280]{2,1,0:T(8,128)(2,1)S(1)} %copy-done.4, s32[1,512]{1,0:T(1,128)S(1)} %copy-done.6, ...), custom_call_target="tpu_custom_call" | custom-call | tf_op jit(solution)/shard_map/pallas_call | solution.py:290
  81.5 0.7 copy.11
  82.2 0.9 %copy.12 = f32[160,1280]{1,0:T(8,128)} copy(f32[160,1280]{1,0:T(8,128)S(1)} %get-tuple-element.5) | data formatting | bytes 1638400
Async XLA Ops:
  0.6 1.9 %copy-start = (bf16[1280,1280]{1,0:T(8,128)(2,1)S(1)}, bf16[1280,1280]{1,0:T(8,128)(2,1)}, u32[]{:S(2)}) copy-start(bf16[1280,1280]{1,0:T(8,128)(2,1)} %w_hbm.1) | copy-start | bytes 9830404
  2.6 1.0 %copy-start.1 = (bf16[1,128,1280]{2,1,0:T(8,128)(2,1)S(1)}, bf16[1,128,1280]{2,1,0:T(8,128)(2,1)}, u32[]{:S(2)}) copy-start(bf16[1,128,1280]{2,1,0:T(8,128)(2,1)} %q_hbm.1) | copy-start | bytes 983044
  3.5 1.0 %copy-start.2 = (bf16[1,128,1280]{2,1,0:T(8,128)(2,1)S(1)}, bf16[1,128,1280]{2,1,0:T(8,128)(2,1)}, u32[]{:S(2)}) copy-start(bf16[1,128,1280]{2,1,0:T(8,128)(2,1)} %k_hbm.1) | copy-start | bytes 983044
  4.5 1.0 %copy-start.3 = (bf16[1,128,1280]{2,1,0:T(8,128)(2,1)S(1)}, bf16[1,128,1280]{2,1,0:T(8,128)(2,1)}, u32[]{:S(2)}) copy-start(bf16[1,128,1280]{2,1,0:T(8,128)(2,1)} %v_hbm.1) | copy-start | bytes 983044
  5.5 1.0 %copy-start.4 = (bf16[1,128,1280]{2,1,0:T(8,128)(2,1)S(1)}, bf16[1,128,1280]{2,1,0:T(8,128)(2,1)}, u32[]{:S(2)}) copy-start(bf16[1,128,1280]{2,1,0:T(8,128)(2,1)} %res_hbm.1) | copy-start | bytes 983044
  6.5 1.0 %copy-start.5 = (bf16[1,128,1280]{2,1,0:T(8,128)(2,1)S(1)}, bf16[1,128,1280]{2,1,0:T(8,128)(2,1)}, u32[]{:S(2)}) copy-start(bf16[1,128,1280]{2,1,0:T(8,128)(2,1)} %cot_hbm.1) | copy-start | bytes 983044
  7.4 0.7 copy-start.6

commit v2 on v1

--- a/solution.py
+++ b/solution.py
@@ -18,7 +18,8 @@
          q, res, cot, w, kbuf, vbuf, cot_t, bias, att, mix, part, dp_in, pair, sec_in, acc,
          chain_out, chain_in,
          local_sem, kv_send, kv_recv, dp_send, dp_recv, sec_send, sec_recv, ch_send, ch_recv):
-    N, S, D, rows, width, C, reach, R, subs = dims
+    N, S, D, rows, width, C, reach, R, step = dims
+    edges = [(lo, min(C, lo + step)) for lo in range(0, C, step)]
     halves = width // C
     head_dim = width // HEADS
     half_heads = C // head_dim
@@ -140,25 +141,35 @@
             out = jnp.dot(expo.astype(jnp.bfloat16), vbuf[:, lo:hi], preferred_element_type=jnp.float32)
             att[:, lo:hi] += out * (mine / total)
 
-    def dp_copy(c, o):
+    def columns(s):
+        return pl.ds(edges[s][0], edges[s][1] - edges[s][0])
+
+    def dp_copy(c, s, o):
         peer = lax.rem(core + o, D)
         return pltpu.make_async_remote_copy(
-            src_ref=part.at[c, peer], dst_ref=dp_in.at[c, o - 1],
-            send_sem=dp_send.at[c, o - 1], recv_sem=dp_recv.at[c, o - 1],
+            src_ref=part.at[c, peer, :, :, columns(s)], dst_ref=dp_in.at[c, o - 1, :, :, columns(s)],
+            send_sem=dp_send.at[c, s, o - 1], recv_sem=dp_recv.at[c, s, o - 1],
             device_id={"dp": peer}, device_id_type=MESH)
 
-    def sec_copy(c, o):
+    def sec_copy(c, s, o):
         peer = lax.rem(sec + o, S)
         return pltpu.make_async_remote_copy(
-            src_ref=pair.at[c, peer], dst_ref=sec_in.at[c, o - 1],
-            send_sem=sec_send.at[c, o - 1], recv_sem=sec_recv.at[c, o - 1],
+            src_ref=pair.at[c, peer, :, columns(s)], dst_ref=sec_in.at[c, o - 1, :, columns(s)],
+            send_sem=sec_send.at[c, s, o - 1], recv_sem=sec_recv.at[c, s, o - 1],
             device_id={"section": peer}, device_id_type=MESH)
+
+    def chain_copy(side, c, s):
+        return pltpu.make_async_remote_copy(
+            src_ref=chain_out.at[side, c, :, columns(s)], dst_ref=chain_in.at[side, c, :, columns(s)],
+            send_sem=ch_send.at[side, c, s], recv_sem=ch_recv.at[side, c, s],
+            device_id={"seq": me + towards[side]}, device_id_type=MESH)
 
     grad_scale = 1.0 / float(S * D * N * rows) ** 0.5
     tile = max(1, 640 // R)
 
-    def partials(c):
-        here = att[:, c * C:(c + 1) * C].astype(jnp.bfloat16)
+    def partials(c, s):
+        lo, hi = edges[s]
+        here = att[:, c * C + lo:c * C + hi].astype(jnp.bfloat16)
         groups = S * D
         for at in range(0, groups, tile):
             count = min(tile, groups - at)
@@ -166,65 +177,56 @@
                             preferred_element_type=jnp.float32) * grad_scale
             for j in range(count):
                 group = at + j
-                part[c, group % D, group // D] = value[j * R:(j + 1) * R].astype(part.dtype)
+                part[c, group % D, group // D, :, lo:hi] = value[j * R:(j + 1) * R].astype(part.dtype)
         for o in range(1, D):
-            dp_copy(c, o).start()
-
-    def pair_up(c):
+            dp_copy(c, s, o).start()
+
+    def pair_up(c, s):
+        lo, hi = edges[s]
         for o in range(1, D):
-            dp_copy(c, o).wait_recv()
+            dp_copy(c, s, o).wait_recv()
         for o in [*range(1, S), 0]:
             peer = lax.rem(sec + o, S)
-            value = part[c, core, peer].astype(jnp.float32)
+            value = part[c, core, peer, :, lo:hi].astype(jnp.float32)
             for p in range(1, D):
-                value = value + dp_in[c, p - 1, peer].astype(jnp.float32)
+                value = value + dp_in[c, p - 1, peer, :, lo:hi].astype(jnp.float32)
             if o:
-                pair[c, peer] = value.astype(pair.dtype)
-                sec_copy(c, o).start()
+                pair[c, peer, :, lo:hi] = value.astype(pair.dtype)
+                sec_copy(c, s, o).start()
             else:
-                acc[c] = value
-
-    edges = [(C // LANES * i // subs * LANES, C // LANES * (i + 1) // subs * LANES) for i in range(subs)]
-
-    def chain_copy(side, c, s):
-        cols = pl.ds(edges[s][0], edges[s][1] - edges[s][0])
-        return pltpu.make_async_remote_copy(
-            src_ref=chain_out.at[side, c, :, cols], dst_ref=chain_in.at[side, c, :, cols],
-            send_sem=ch_send.at[side, c, s], recv_sem=ch_recv.at[side, c, s],
-            device_id={"seq": me + towards[side]}, device_id_type=MESH)
-
-    def chain_start(c):
+                acc[c, :, lo:hi] = value
+
+    def chain_start(c, s):
+        lo, hi = edges[s]
         for o in range(1, S):
-            sec_copy(c, o).wait_recv()
-        for s, (lo, hi) in enumerate(edges):
-            value = acc[c, :, lo:hi]
-            for o in range(1, S):
-                value = value + sec_in[c, o - 1, :, lo:hi].astype(jnp.float32)
-            acc[c, :, lo:hi] = value
-            for side in range(2):
-                @pl.when(can_send(towards[side]) & jnp.logical_not(can_take(towards[side], 1)))
+            sec_copy(c, s, o).wait_recv()
+        value = acc[c, :, lo:hi]
+        for o in range(1, S):
+            value = value + sec_in[c, o - 1, :, lo:hi].astype(jnp.float32)
+        acc[c, :, lo:hi] = value
+        for side in range(2):
+            @pl.when(can_send(towards[side]) & jnp.logical_not(can_take(towards[side], 1)))
+            def _():
+                chain_out[side, c, :, lo:hi] = acc[c, :, lo:hi].astype(chain_out.dtype)
+                chain_copy(side, c, s).start()
+        wg_ref[:, c * C + lo:c * C + hi] = value
+
+    def chain_step(c, s, turn):
+        lo, hi = edges[s]
+        for side in range(2):
+            near = (me * 2 < N) if side == 0 else (me * 2 >= N)
+            now = near if turn == 0 else jnp.logical_not(near)
+
+            @pl.when(now & can_take(towards[side], 1))
+            def _():
+                chain_copy(side, c, s).wait_recv()
+                came = chain_in[side, c, :, lo:hi].astype(jnp.float32)
+
+                @pl.when(can_send(towards[side]))
                 def _():
-                    chain_out[side, c, :, lo:hi] = acc[c, :, lo:hi].astype(chain_out.dtype)
+                    chain_out[side, c, :, lo:hi] = (acc[c, :, lo:hi] + came).astype(chain_out.dtype)
                     chain_copy(side, c, s).start()
-            wg_ref[:, c * C + lo:c * C + hi] = value
-
-    def chain_rest(c):
-        for s, (lo, hi) in enumerate(edges):
-            for turn in range(2):
-                for side in range(2):
-                    near = (me * 2 < N) if side == 0 else (me * 2 >= N)
-                    now = near if turn == 0 else jnp.logical_not(near)
-
-                    @pl.when(now & can_take(towards[side], 1))
-                    def _():
-                        chain_copy(side, c, s).wait_recv()
-                        came = chain_in[side, c, :, lo:hi].astype(jnp.float32)
-
-                        @pl.when(can_send(towards[side]))
-                        def _():
-                            chain_out[side, c, :, lo:hi] = (acc[c, :, lo:hi] + came).astype(chain_out.dtype)
-                            chain_copy(side, c, s).start()
-                        wg_ref[:, c * C + lo:c * C + hi] += came
+                wg_ref[:, c * C + lo:c * C + hi] += came
 
     def project(c):
         here = att[:, c * C:(c + 1) * C].astype(jnp.bfloat16)
@@ -237,19 +239,25 @@
         if c == halves - 1:
             mix_ref[0] = (mix[...] + (value if c else 0.0)).astype(mix_ref.dtype)
 
+    pieces = [(c, s) for c in range(halves) for s in range(len(edges))]
     for c in range(halves):
         attention(c)
-        partials(c)
+        for s in range(len(edges)):
+            partials(c, s)
         if c == 0:
             for copy in locals_[4:]:
                 copy.wait()
         if c < halves - 1:
             project(c)
-        pair_up(c)
+        for s in range(len(edges)):
+            pair_up(c, s)
     project(halves - 1)
-    for c in range(halves):
-        chain_start(c)
-        chain_rest(c)
+    for at in range(len(pieces) + 1):
+        if at < len(pieces):
+            chain_start(*pieces[at])
+            chain_step(*pieces[at], 0)
+        if at > 0:
+            chain_step(*pieces[at - 1], 1)
 
     for c in range(halves):
         for side in range(2):
@@ -261,12 +269,13 @@
 
             @pl.when(can_send(towards[side]))
             def _():
-                for s in range(subs):
+                for s in range(len(edges)):
                     chain_copy(side, c, s).wait_send()
-        for o in range(1, D):
-            dp_copy(c, o).wait_send()
-        for o in range(1, S):
-            sec_copy(c, o).wait_send()
+        for s in range(len(edges)):
+            for o in range(1, D):
+                dp_copy(c, s, o).wait_send()
+            for o in range(1, S):
+                sec_copy(c, s, o).wait_send()
 
 
 def solution(mesh):
@@ -279,7 +288,8 @@
         halves = width // C
         reach = min(-(-(MOST - 1) // rows), N - 1)
         R = width // (S * D)
-        subs = 2
+        step = C
+        subs = -(-C // step)
         link = jnp.bfloat16 if N <= 8 else jnp.float32
         bf, f32 = jnp.bfloat16, jnp.float32
         span = (2 * reach + 1) * rows
@@ -288,7 +298,7 @@
         anywhere = pl.BlockSpec(memory_space=pl.ANY)
         vmem = pl.BlockSpec(memory_space=pltpu.VMEM)
         return pl.pallas_call(
-            functools.partial(body, (N, S, D, rows, width, C, reach, R, subs)),
+            functools.partial(body, (N, S, D, rows, width, C, reach, R, step)),
             out_shape=(jax.ShapeDtypeStruct((1, rows, width), bf), jax.ShapeDtypeStruct((R, width), f32)),
             in_specs=[anywhere] * 4 + [vmem] + [anywhere] * 2,
             out_specs=(vmem, vmem),
@@ -303,11 +313,12 @@
                 pltpu.VMEM((halves, R, C), f32),
                 pltpu.VMEM((2, halves, R, C), link), pltpu.VMEM((2, halves, R, C), link),
                 dma((6,)), dma((2, reach, halves, 2)), dma((2, reach, halves, 2)),
-                dma((halves, cores)), dma((halves, cores)), dma((halves, others)), dma((halves, others)),
+                dma((halves, subs, cores)), dma((halves, subs, cores)),
+                dma((halves, subs, others)), dma((halves, subs, others)),
                 dma((2, halves, subs)), dma((2, halves, subs)),
             ],
             compiler_params=pltpu.CompilerParams(
-                collective_id=0, has_side_effects=True, vmem_limit_bytes=48 * 1024 * 1024),
+                collective_id=0, has_side_effects=True, vmem_limit_bytes=62 * 1024 * 1024),
         )(queries, key_input, value_input, residual, segments, out_weight, cotangent)
 
     rows_spec = P(("section", "dp"), "seq", None)

time: 83.5 us -> 77.2 us (0.925)
  local copies, waits for them, and re-layouts: 9.08 us -> 3.81 us
  Pallas kernels: 73.4 us -> 72.5 us
    unnamed x16 -> x2, local copies, waits for them, and re-layouts: 9.08 us -> 3.81 us
    pallas_call x1, Pallas kernels: 73.4 us -> 72.5 us  [per_device(): pl.pallas_call(functools.partial(body, (N, S, D, rows, width, C, reach, R...]
where the time goes in v2:
time: 77.2 us; the launch traced here: 77 us
  Pallas kernels  72.5 us (94%)
  local copies, waits for them, and re-layouts  3.81 us (5%)
    pallas_call x1, Pallas kernels, per_device(): pl.pallas_call(functools.partial(body, (N, S, D, rows, width, C, reach, R...  72.5 us
    unnamed x2, local copies, waits for them, and re-layouts  3.81 us

profile of v2, /device:TPU:0, one launch (start us, length us, event | category | flops | bytes accessed | tf_op | source)
XLA Modules:
  0.0 77.0 jit_solution(7691461237418227842)
XLA Ops:
  0.6 72.5 %shard_map.86 = (bf16[1,128,1280]{2,1,0:T(8,128)(2,1)}, f32[160,1280]{1,0:T(8,128)}) custom-call(bf16[1,128,1280]{2,1,0:T(8,128)(2,1)} %q_hbm.1, bf16[1,128,1280]{2,1,0:T(8,128)(2,1)} %k_hbm.1, bf16[1,128,1280]{2,1,0:T(8,128)(2,1)} %v_hbm.1, bf16[1,128,1280]{2,1,0:T(8,128)(2,1)} %res_hbm.1, s32[1,512]{1,0:T(1,128)} %seg_ref.1, bf16[1280,1280]{1,0:T(8,128)(2,1)} %w_hbm.1, ...), custom_call_target="tpu_custom_call" | custom-call | tf_op jit(solution)/shard_map/pallas_call | solution.py:300
  73.2 1.7 %copy.11 = bf16[1,128,1280]{2,1,0:T(8,128)(2,1)} copy(bf16[1,128,1280]{2,1,0:T(8,128)(2,1)} %get-tuple-element.4) | data formatting | bytes 655360
  74.9 2.1 %copy.12 = f32[160,1280]{1,0:T(8,128)} copy(f32[160,1280]{1,0:T(8,128)} %get-tuple-element.5) | data formatting | bytes 1638400

commit v3 on v2

--- a/solution.py
+++ b/solution.py
@@ -255,9 +255,10 @@
     for at in range(len(pieces) + 1):
         if at < len(pieces):
             chain_start(*pieces[at])
-            chain_step(*pieces[at], 0)
         if at > 0:
             chain_step(*pieces[at - 1], 1)
+        if at < len(pieces):
+            chain_step(*pieces[at], 0)
 
     for c in range(halves):
         for side in range(2):

time: 77.2 us -> 77.2 us (level)
  no operation moved by 1% of the time
where the time goes in v3:
time: 77.2 us; the launch traced here: 77 us
  Pallas kernels  72.5 us (94%)
  local copies, waits for them, and re-layouts  3.81 us (5%)
    pallas_call x1, Pallas kernels, per_device(): pl.pallas_call(functools.partial(body, (N, S, D, rows, width, C, reach, R...  72.5 us
    unnamed x2, local copies, waits for them, and re-layouts  3.81 us

profile of v3, /device:TPU:0, one launch (start us, length us, event | category | flops | bytes accessed | tf_op | source)
XLA Modules:
  0.0 77.0 jit_solution(9613174569902999465)
XLA Ops:
  0.6 72.5 %shard_map.86 = (bf16[1,128,1280]{2,1,0:T(8,128)(2,1)}, f32[160,1280]{1,0:T(8,128)}) custom-call(bf16[1,128,1280]{2,1,0:T(8,128)(2,1)} %q_hbm.1, bf16[1,128,1280]{2,1,0:T(8,128)(2,1)} %k_hbm.1, bf16[1,128,1280]{2,1,0:T(8,128)(2,1)} %v_hbm.1, bf16[1,128,1280]{2,1,0:T(8,128)(2,1)} %res_hbm.1, s32[1,512]{1,0:T(1,128)} %seg_ref.1, bf16[1280,1280]{1,0:T(8,128)(2,1)} %w_hbm.1, ...), custom_call_target="tpu_custom_call" | custom-call | tf_op jit(solution)/shard_map/pallas_call | solution.py:301
  73.2 1.7 %copy.11 = bf16[1,128,1280]{2,1,0:T(8,128)(2,1)} copy(bf16[1,128,1280]{2,1,0:T(8,128)(2,1)} %get-tuple-element.4) | data formatting | bytes 655360
  74.9 2.1 %copy.12 = f32[160,1280]{1,0:T(8,128)} copy(f32[160,1280]{1,0:T(8,128)} %get-tuple-element.5) | data formatting | bytes 1638400
